TPU v7x, 128 devices: a whole 4x4x4 slice. The times are simulated.
128 devices in a mesh: section: 2 (over core), row: 16 (over z, y), col: 4 (over x).
Axes of the slice: x: 4, y: 4, z: 4, core: 2. Of those that a mesh axis runs over, the one named last changes fastest.
Arguments:
- ends: bfloat16 [2, 2, 3152, 768], P('section', None, 'row', 'col'), may hold values from -6 to 6
- gain_attn: float32 [2, 768], P('section'), may hold values from 0.5 to 1.5
- w_qkv: bfloat16 [2, 768, 2304], P('section', 'row', 'col'), may hold values from -0.21875 to 0.21875
- w_out: bfloat16 [2, 768, 768], P('section', 'col', 'row'), may hold values from -1.75 to 1.75
- gain_ffn: float32 [2, 768], P('section'), may hold values from 0.5 to 1.5
- w_fc1: bfloat16 [768, 3072], P('row', ('section', 'col')), may hold values from -0.21875 to 0.21875
- w_fc2: bfloat16 [3072, 768], P(('section', 'col'), 'row'), may hold values from -0.15625 to 0.15625
- router: bfloat16 [768, 16], P('section'), may hold values from -0.15625 to 0.15625
- w_up: bfloat16 [16, 768, 3072], P('row', 'section', 'col'), may hold values from -0.21875 to 0.21875
- w_down: bfloat16 [16, 3072, 768], P('row', 'col', 'section'), may hold values from -1.75 to 1.75
- routes: int32 [2, 3152, 2], P(None, 'row'), may hold values from 0 to 15, all different within a row; in each aligned block of 197 rows (0 to 196, 197 to 393, ..., all dimensions but the last counted through in order) at most 40 rows name the same one
Outputs:
- ends_out: bfloat16 [2, 2, 3152, 768], P('section', None, 'row', 'col')
- grad_gain_attn: float32 [2, 768], P('section')
- grad_w_qkv: float32 [2, 768, 2304], P('section', 'row', 'col')
- grad_w_out: float32 [2, 768, 768], P('section', 'col', 'row')
- grad_gain_ffn: float32 [2, 768], P('section')
- grad_w_fc1: float32 [768, 3072], P('row', ('section', 'col'))
- grad_w_fc2: float32 [3072, 768], P(('section', 'col'), 'row')
- grad_router: float32 [768, 16], P('section')
- grad_w_up: float32 [16, 768, 3072], P('row', 'section', 'col')
- grad_w_down: float32 [16, 3072, 768], P('row', 'col', 'section')
Inputs may be any that keep to these rules, and one draw needn't show every extreme that they name: `routes`: each token names 2 different experts. Among the 197 tokens of one index of row in one micro-batch (aligned blocks of 197 tokens), no expert is named more than 40 times, a bound that some block reaches in every draw.
All inputs are finite; a program needn't handle non-finite values.
Results may differ from a plain program's by a relative error of at most 0.035.
Values may be sent and summed in bfloat16 or wider, within the bound.
No kernel may reach another device: no remote copies, remote signals or barrier semaphores. Data moves between devices by JAX's collectives and lax.ppermute only.
A program may use at most 192 MiB of HBM per device.

v0:
```python
import jax
import jax.numpy as jnp
from jax import lax
from jax.sharding import PartitionSpec as P

HD = 64
SEQ = 197


exact_mode = lax.Precision.HIGHEST


def passed_along(block, axis, distance):
    devices = range(lax.axis_size(axis))
    route = [(i - distance, i) for i in devices if i - distance in devices]
    return lax.ppermute(block, axis, route)


def norm_rows(values, gain):
    centre = values - jnp.mean(values, axis=-1, keepdims=True)
    spread = jnp.mean(centre * centre, axis=-1, keepdims=True)
    return centre * lax.rsqrt(spread + 1e-06) * gain


def gelu_exact(values):
    return jax.nn.gelu(values, approximate=False)


def matmul(left, right):
    return jnp.dot(left, right, preferred_element_type=jnp.float32)


def matmul_left_t(left, right):
    return lax.dot_general(
        left, right, (((0,), (0,)), ((), ())), preferred_element_type=jnp.float32
    )


def matmul_right_t(left, right):
    return lax.dot_general(
        left, right, (((1,), (1,)), ((), ())), preferred_element_type=jnp.float32
    )


def gate_values(logits, choices):
    return jnp.take_along_axis(jax.nn.softmax(logits, axis=-1), choices, axis=1)


def gather_features(values):
    return lax.all_gather(values, "col", axis=1, tiled=True)


def sum_features(values):
    return lax.psum_scatter(
        values.astype(jnp.bfloat16), "col", scatter_dimension=1, tiled=True
    ).astype(jnp.float32)


def toward_experts(values):
    return lax.all_to_all(values, "row", split_axis=0, concat_axis=0, tiled=True)


def return_rows(values):
    return lax.all_to_all(values, "row", split_axis=0, concat_axis=0, tiled=True)


def route_table(choices, experts, capacity):
    flat = choices.reshape(-1)
    onehot = (flat[:, None] == jnp.arange(experts, dtype=jnp.int32)[None, :]).astype(jnp.int32)
    placed = jnp.sum((jnp.cumsum(onehot, axis=0) - 1) * onehot, axis=1)
    target = flat * capacity + placed
    owners = jnp.repeat(jnp.arange(choices.shape[0], dtype=jnp.int32), choices.shape[1])
    slot_token = jnp.zeros((experts * capacity,), jnp.int32).at[target].set(owners)
    slot_used = jnp.zeros((experts * capacity,), jnp.float32).at[target].set(1.0)
    return (target, slot_token, slot_used)


def body(ends, gain_attn, w_qkv, w_out, gain_ffn, w_fc1, w_fc2, router, w_up, w_down, routes):
    batches = ends.shape[1]
    tokens_here = ends.shape[2]
    quarter = ends.shape[3]
    experts = router.shape[1]
    choices_per = routes.shape[2]
    capacity = 8 * (3 * tokens_here * choices_per // (2 * experts * 8) + 1)
    column = lax.axis_index("col")
    first = lax.axis_index("section") == 0
    on_first = jnp.where(first, 1.0, 0.0).astype(jnp.float32)
    on_second = 1.0 - on_first
    fc_in_part, fc_out_part, gate_table, up_block, down_block = (
        lax.all_gather(w_fc1, "section", axis=1, tiled=True),
        lax.all_gather(w_fc2, "section", axis=0, tiled=True),
        lax.all_gather(router, "section", axis=0, tiled=True),
        lax.all_gather(w_up[0], "section", axis=0, tiled=True),
        lax.all_gather(w_down[0], "section", axis=1, tiled=True),
    )
    attn_cols, out_rows, fc_in, fc_out = (
        lax.all_gather(w_qkv[0], "row", axis=0, tiled=True),
        lax.all_gather(w_out[0], "row", axis=1, tiled=True),
        lax.all_gather(fc_in_part, "row", axis=0, tiled=True),
        lax.all_gather(fc_out_part, "row", axis=1, tiled=True),
    )
    heads_here = attn_cols.shape[1] // (3 * HD)
    images = tokens_here // SEQ
    scale = HD ** (-0.5)
    gain_one = gain_attn[0]
    gain_two = gain_ffn[0]

    def forward(inputs_b, choices):
        whole = gather_features(inputs_b)
        normed = norm_rows(whole.astype(jnp.float32), gain_one).astype(jnp.bfloat16)
        project = matmul(normed, attn_cols).astype(jnp.bfloat16)
        parts = project.reshape(images, SEQ, heads_here, 3, HD)
        scores = (
            jnp.einsum(
                "bqhd,bkhd->bhqk",
                parts[:, :, :, 0],
                parts[:, :, :, 1],
                preferred_element_type=jnp.float32,
            )
            * scale
        )
        log_total = jax.nn.logsumexp(scores, axis=-1, keepdims=True)
        weights = jnp.exp(scores - log_total).astype(jnp.bfloat16)
        mixed = jnp.einsum(
            "bhqk,bkhd->bqhd", weights, parts[:, :, :, 2], preferred_element_type=jnp.float32
        )
        mixed = mixed.astype(jnp.bfloat16).reshape(tokens_here, heads_here * HD)
        middle = inputs_b.astype(jnp.float32) + sum_features(matmul(mixed, out_rows))
        second_in = gather_features(middle.astype(jnp.bfloat16)).astype(jnp.float32)
        second = norm_rows(second_in, gain_two).astype(jnp.bfloat16)
        fc_hidden = matmul(second, fc_in)
        fc_active = gelu_exact(fc_hidden).astype(jnp.bfloat16)
        dense_out = sum_features(matmul(fc_active, fc_out))
        logits = matmul(second, gate_table)
        gates = gate_values(logits, choices)
        target, slot_token, slot_used = route_table(choices, experts, capacity)
        own = lax.dynamic_slice_in_dim(second, column * quarter, quarter, 1)
        outgoing = (own[slot_token].astype(jnp.float32) * slot_used[:, None]).astype(jnp.bfloat16)
        arrived = toward_experts(outgoing.reshape(experts, capacity, quarter))
        rows = gather_features(arrived.reshape(-1, quarter))
        hidden = matmul(rows, up_block)
        active = gelu_exact(hidden).astype(jnp.bfloat16)
        result = sum_features(matmul(active, down_block)).astype(jnp.bfloat16)
        back = return_rows(result.reshape(-1, capacity, quarter)).reshape(
            experts * capacity, quarter
        )
        picked = back[target].astype(jnp.float32).reshape(tokens_here, choices_per, quarter)
        expert_out = jnp.sum(gates[:, :, None] * picked, axis=1)
        outputs = middle + jnp.where(first, dense_out, expert_out)
        kept = (
            whole,
            normed,
            project,
            log_total,
            mixed,
            second_in,
            second,
            logits,
            gates,
            choices,
            target,
            slot_token,
            rows,
            hidden,
            active,
            picked,
            fc_hidden,
            fc_active,
        )
        return (outputs, kept)

    def backward(kept, grad_out):
        (
            whole,
            normed,
            project,
            log_total,
            mixed,
            second_in,
            second,
            logits,
            gates,
            choices,
            target,
            slot_token,
            rows,
            hidden,
            active,
            picked,
            fc_hidden,
            fc_active,
        ) = kept
        grad_gates = jnp.sum(grad_out[:, None, :] * picked, axis=2)
        slot_gate = jnp.zeros((experts * capacity,), jnp.float32).at[target].set(gates.reshape(-1))
        grad_slots = (grad_out[slot_token] * slot_gate[:, None]).astype(jnp.bfloat16)
        grad_arrived = toward_experts(grad_slots.reshape(experts, capacity, quarter))
        grad_result = gather_features(grad_arrived.reshape(-1, quarter))
        grad_down = matmul_left_t(active, grad_result)
        grad_active = matmul_right_t(grad_result, down_block)
        grad_hidden = jax.vjp(gelu_exact, hidden)[1](grad_active)[0].astype(jnp.bfloat16)
        grad_up = matmul_left_t(rows, grad_hidden)
        grad_rows = sum_features(matmul_right_t(grad_hidden, up_block)).astype(jnp.bfloat16)
        grad_back = return_rows(grad_rows.reshape(-1, capacity, quarter)).reshape(
            experts * capacity, quarter
        )
        grad_own = jnp.sum(
            grad_back[target].astype(jnp.float32).reshape(tokens_here, choices_per, quarter), axis=1
        )

        def gate_part(values):
            return gate_values(values, choices)

        grad_logits = jax.vjp(gate_part, logits)[1](grad_gates)[0]
        second_float = second.astype(jnp.float32)
        table_float = gate_table.astype(jnp.float32)
        grad_router = jnp.dot(second_float.T, grad_logits, precision=exact_mode)
        grad_expert_side = jnp.dot(grad_logits, table_float.T, precision=exact_mode)
        mine = lax.dynamic_slice_in_dim(grad_expert_side, column * quarter, quarter, 1) + grad_own
        grad_expert_side = lax.dynamic_update_slice_in_dim(
            grad_expert_side, mine, column * quarter, 1
        )
        grad_dense = gather_features(grad_out.astype(jnp.bfloat16))
        grad_fc_out = matmul_left_t(fc_active, grad_dense)
        grad_fc_active = matmul_right_t(grad_dense, fc_out)
        grad_fc_hidden = jax.vjp(gelu_exact, fc_hidden)[1](grad_fc_active)[0].astype(jnp.bfloat16)
        grad_fc_in = matmul_left_t(second, grad_fc_hidden)
        grad_dense_side = matmul_right_t(grad_fc_hidden, fc_in)
        grad_second = jnp.where(first, grad_dense_side, grad_expert_side)
        grad_middle_part, grad_gain_two = jax.vjp(norm_rows, second_in, gain_two)[1](grad_second)
        grad_middle = grad_out + sum_features(grad_middle_part)
        grad_branch = gather_features(grad_middle.astype(jnp.bfloat16))
        grad_out_rows = matmul_left_t(mixed, grad_branch)
        grad_mixed = matmul_right_t(grad_branch, out_rows).astype(jnp.bfloat16)
        grad_mixed = grad_mixed.reshape(images, SEQ, heads_here, HD)
        parts = project.reshape(images, SEQ, heads_here, 3, HD)
        queries = parts[:, :, :, 0]
        keys = parts[:, :, :, 1]
        values = parts[:, :, :, 2]
        scores = (
            jnp.einsum("bqhd,bkhd->bhqk", queries, keys, preferred_element_type=jnp.float32) * scale
        )
        shares = jnp.exp(scores - log_total)
        weights = shares.astype(jnp.bfloat16)
        grad_weights = jnp.einsum(
            "bqhd,bkhd->bhqk", grad_mixed, values, preferred_element_type=jnp.float32
        )
        grad_values = jnp.einsum(
            "bhqk,bqhd->bkhd", weights, grad_mixed, preferred_element_type=jnp.float32
        )
        grad_scores = shares * (
            grad_weights - jnp.sum(grad_weights * shares, axis=-1, keepdims=True)
        )
        grad_scores = grad_scores.astype(jnp.bfloat16)
        grad_queries = (
            jnp.einsum("bhqk,bkhd->bqhd", grad_scores, keys, preferred_element_type=jnp.float32)
            * scale
        )
        grad_keys = (
            jnp.einsum("bhqk,bqhd->bkhd", grad_scores, queries, preferred_element_type=jnp.float32)
            * scale
        )
        grad_project = jnp.stack([grad_queries, grad_keys, grad_values], axis=3).astype(
            jnp.bfloat16
        )
        grad_project = grad_project.reshape(tokens_here, -1)
        grad_attn_cols = matmul_left_t(normed, grad_project)
        grad_normed = matmul_right_t(grad_project, attn_cols)
        grad_whole_part, grad_gain_one = jax.vjp(norm_rows, whole.astype(jnp.float32), gain_one)[1](
            grad_normed
        )
        grad_inputs = grad_middle + sum_features(grad_whole_part)
        terms = (
            grad_attn_cols,
            grad_out_rows,
            grad_fc_in * on_first,
            grad_fc_out * on_first,
            grad_up * on_second,
            grad_down * on_second,
            grad_gain_one,
            grad_gain_two,
            grad_router * on_second,
        )
        return (grad_inputs, terms)

    results = []
    kept_list = []
    incoming = jnp.zeros((tokens_here, quarter), jnp.bfloat16)
    for moment in range(batches + 1):
        early = min(moment, batches - 1)
        late = max(moment - 1, 0)
        inputs_b = jnp.where(first, ends[0, early], incoming)
        choices = routes[late]
        outputs, kept = forward(inputs_b, choices)
        outputs_b = outputs.astype(jnp.bfloat16)
        results.append(outputs_b)
        kept_list.append((inputs_b, choices))
        if moment < batches:
            incoming = passed_along(outputs_b, "section", 1)
    totals = None
    returned_grads = []
    grads_in = jnp.zeros((tokens_here, quarter), jnp.float32)
    for moment in range(batches + 1):
        later = min(moment + 1, batches)
        earlier = max(moment - 1, 0)

        def pick_section(former, latter):
            return jnp.where(first, former, latter)

        restored = jax.tree.map(pick_section, kept_list[earlier], kept_list[later])
        restored = forward(restored[0], restored[1])[1]
        live = 1.0 if moment < batches else 0.0
        cotangent = ends[0, min(moment, batches - 1)].astype(jnp.float32) * live
        grad_out = jnp.where(first, grads_in, cotangent)
        grad_inputs, terms = backward(restored, grad_out)
        grad_inputs_b = grad_inputs.astype(jnp.bfloat16)
        returned_grads.append(grad_inputs_b)
        if moment < batches:
            grads_in = passed_along(grad_inputs_b, "section", -1).astype(jnp.float32)
        if totals is None:
            totals = terms
        else:
            totals = jax.tree.map(jnp.add, totals, terms)
    shared = (
        lax.psum_scatter(
            totals[0].astype(jnp.bfloat16), "row", scatter_dimension=0, tiled=True
        ).astype(jnp.float32),
        lax.psum_scatter(
            totals[1].astype(jnp.bfloat16), "row", scatter_dimension=1, tiled=True
        ).astype(jnp.float32),
        lax.psum_scatter(
            totals[2].astype(jnp.bfloat16), "row", scatter_dimension=0, tiled=True
        ).astype(jnp.float32),
        lax.psum_scatter(
            totals[3].astype(jnp.bfloat16), "row", scatter_dimension=1, tiled=True
        ).astype(jnp.float32),
    )
    small = lax.psum((totals[6], totals[7], totals[8]), ("row", "col"))
    halves = (
        lax.psum_scatter(
            shared[2].astype(jnp.bfloat16), "section", scatter_dimension=1, tiled=True
        ).astype(jnp.float32),
        lax.psum_scatter(
            shared[3].astype(jnp.bfloat16), "section", scatter_dimension=0, tiled=True
        ).astype(jnp.float32),
        lax.psum_scatter(
            small[2].astype(jnp.bfloat16), "section", scatter_dimension=0, tiled=True
        ).astype(jnp.float32),
        lax.psum_scatter(
            totals[4].astype(jnp.bfloat16), "section", scatter_dimension=0, tiled=True
        ).astype(jnp.float32),
        lax.psum_scatter(
            totals[5].astype(jnp.bfloat16), "section", scatter_dimension=1, tiled=True
        ).astype(jnp.float32),
    )
    ends_out = jnp.stack(
        [
            jnp.where(first, returned_grads[batch + 1], results[batch + 1])
            for batch in range(batches)
        ]
    )[None]
    return (
        ends_out,
        small[0][None],
        shared[0][None],
        shared[1][None],
        small[1][None],
        halves[0],
        halves[1],
        halves[2],
        halves[3][None],
        halves[4][None],
    )


def solution(mesh):
    placed = (
        P("section", None, "row", "col"),
        P("section", None),
        P("section", "row", "col"),
        P("section", "col", "row"),
        P("section", None),
        P("row", ("section", "col")),
        P(("section", "col"), "row"),
        P("section", None),
        P("row", "section", "col"),
        P("row", "col", "section"),
        P(None, "row", None),
    )
    return jax.shard_map(
        body,
        mesh=mesh,
        in_specs=placed,
        out_specs=(
            P("section", None, "row", "col"),
            P("section", None),
            P("section", "row", "col"),
            P("section", "col", "row"),
            P("section", None),
            P("row", ("section", "col")),
            P(("section", "col"), "row"),
            P("section", None),
            P("row", "section", "col"),
            P("row", "col", "section"),
        ),
        check_vma=False,
    )
```

profile of v0, /device:TPU:0, one launch (start us, length us, event | category | flops | bytes accessed | tf_op | source)
XLA Modules:
  0.0 1778.9 jit_solution(3977128283869775515)
XLA Ops:
  8.1 26.5 %all-gather.1 = bf16[1,768,576]{2,1,0:T(8,128)(2,1)S(1)} all-gather(bf16[1,48,576]{2,1,0:T(8,128)(2,1)} %param.15), channel_id=3, replica_groups=mesh['section'=2,'row'=16,'col'=4] {'row'}, dimensions={1}, use_global_device_ids=true | all-gather | bytes 940032 | tf_op jit(solution)/shard_map/all_gather | solution.py:97
  35.5 12.9 all-gather
  50.3 23.0 %all-gather.2 = bf16[1,192,768]{1,2,0:T(8,128)(2,1)S(1)} all-gather(bf16[1,192,48]{1,2,0:T(8,128)(2,1)S(1)} %copy-done.186), channel_id=4, replica_groups=mesh['section'=2,'row'=16,'col'=4] {'row'}, dimensions={2}, use_global_device_ids=true | all-gather | bytes 313344 | tf_op jit(solution)/shard_map/all_gather | solution.py:98
  127.4 15.8 all_gather.117
  156.3 36.7 %all-gather.10.cloned.1.call-done = bf16[768,768]{1,0:T(8,128)(2,1)} async-done(((bf16[48,768]{1,0:T(8,128)(2,1)}), bf16[768,768]{1,0:T(8,128)(2,1)}) %all-gather.10.cloned.1.call-update) | async-done | bytes 1179664 | tf_op jit(solution)/shard_map/all_gather | solution.py:99
  225.6 13.2 all_gather.120
  243.0 13.1 all_gather.126
  325.3 14.0 all_gather.128
  347.9 16.2 all_gather.123
  381.9 14.5 all_gather.122
  438.8 21.9 %scatter_fusion = f32[197,16]{0,1:T(8,128)S(1)} fusion(f32[197,16]{0,1:T(8,128)S(1)} %broadcast_in_dim.82.clone, s32[394]{0:T(512)S(1)} %reshape.1672, f32[394]{0:T(512)S(1)} %reshape.1674), kind=kCustom, calls=%fused_computation.33 | custom fusion | flops 394 | bytes 7880 | tf_op jit(solution)/shard_map/transpose(jvp(jit(take_along_axis)))/scatter-add | solution.py:46
  495.6 13.0 all_gather.135
  541.8 14.6 all_gather.124
  564.9 12.9 all_gather.142
  578.8 16.4 reduce-scatter.76.cloned.1.call-done
  608.6 14.2 all_gather.136
  675.6 15.5 all_gather.132
  737.0 15.3 reduce-scatter.68.cloned.1.call-done
  772.9 21.9 %scatter_fusion.1 = f32[197,16]{0,1:T(8,128)S(1)} fusion(f32[197,16]{0,1:T(8,128)S(1)} %broadcast_in_dim.82.clone.1, s32[394]{0:T(512)S(1)} %reshape.1678, f32[394]{0:T(512)S(1)} %reshape.1680), kind=kCustom, calls=%fused_computation.34 | custom fusion | flops 394 | bytes 7880 | tf_op jit(solution)/shard_map/transpose(jvp(jit(take_along_axis)))/scatter-add | solution.py:46
  816.5 14.8 all_gather.133
  839.2 13.3 all_gather.131
  897.5 15.4 all_gather.138
  983.0 15.3 all_gather.139
  1008.4 14.2 all_gather.137
  1063.1 14.8 all_gather.143
  1080.8 21.9 %scatter_fusion.2 = f32[197,16]{0,1:T(8,128)S(1)} fusion(f32[197,16]{0,1:T(8,128)S(1)} %broadcast_in_dim.82, s32[394]{0:T(512)S(1)} %reshape.1678, f32[394]{0:T(512)S(1)} %reshape.1686), kind=kCustom, calls=%fused_computation.35 | custom fusion | flops 394 | bytes 7880 | tf_op jit(solution)/shard_map/transpose(jvp(jit(take_along_axis)))/scatter-add | solution.py:46
  1152.6 26.1 %reduce-scatter.102.cloned.1.call-done = bf16[48,768]{1,0:T(8,128)(2,1)} async-done(((bf16[768,768]{1,0:T(8,128)(2,1)}), bf16[48,768]{1,0:T(8,128)(2,1)}) %reduce-scatter.102.cloned.1.call-update) | async-done | bytes 73744
  1219.1 347.4 %all-reduce.4 = (f32[1,768]{1,0:T(1,128)}, f32[1,768]{1,0:T(1,128)}, bf16[768,16]{0,1:T(8,128)(2,1)S(1)}) all-reduce(f32[1,768]{1,0:T(1,128)S(1)} %broadcast_in_dim.101, f32[1,768]{1,0:T(1,128)S(1)} %broadcast_in_dim.106, f32[768,16]{0,1:T(8,128)S(1)} %fusion.103), channel_id=1, replica_groups=mesh['section'=2,'row'=16,'col'=4] {'row','col'}, use_global_device_ids=true, to_apply=%region_123.125 | all-reduce | flops 13824 | bytes 86016 | tf_op jit(solution)/shard_map/psum | solution.py:337
  1607.2 40.7 %reduce-scatter.92.cloned.1.call-done = bf16[192,48]{0,1:T(8,128)(2,1)} async-done(((bf16[192,768]{0,1:T(8,128)(2,1)}), bf16[192,48]{0,1:T(8,128)(2,1)}) %reduce-scatter.92.cloned.1.call-update) | async-done | bytes 18448 | tf_op jit(solution)/shard_map/reduce_scatter | solution.py:327
  1649.2 21.2 %reduce-scatter.88.cloned.1.call-done = bf16[197,192]{0,1:T(8,128)(2,1)} async-done(((bf16[197,768]{0,1:T(8,128)(2,1)}), bf16[197,192]{0,1:T(8,128)(2,1)}) %reduce-scatter.88.cloned.1.call-update) | async-done | bytes 75664 | tf_op jit(solution)/shard_map/reduce_scatter | solution.py:54
  1670.5 23.1 %reduce-scatter.84.cloned.1.call-done = bf16[197,192]{0,1:T(8,128)(2,1)} async-done(((bf16[197,768]{0,1:T(8,128)(2,1)}), bf16[197,192]{0,1:T(8,128)(2,1)}) %reduce-scatter.84.cloned.1.call-update) | async-done | bytes 75664 | tf_op jit(solution)/shard_map/reduce_scatter | solution.py:54
  1695.3 74.0 %reduce-scatter.108.cloned.1.call-done = bf16[48,576]{1,0:T(8,128)(2,1)} async-done(((bf16[768,576]{1,0:T(8,128)(2,1)}), bf16[48,576]{1,0:T(8,128)(2,1)}) %reduce-scatter.108.cloned.1.call-update) | async-done | bytes 55312
  (1099 shorter events, 784.0 us)
Async XLA Ops:
  8.0 85.4 %reduce-scatter.44.cloned.1.call-start = ((), (), s32[]{:S(2)}) async-start(), calls=%async_computation.51 | async-start | bytes 491520 | tf_op jit(solution)/shard_map/reduce_scatter | solution.py:54
  74.3 68.9 %all-gather.16.cloned.1.call-start = ((), (), s32[]{:S(2)}) async-start(), calls=%async_computation.82 | async-start | bytes 1769472 | tf_op jit(solution)/shard_map/all_gather | solution.py:94
  74.9 68.3 %all-gather.14.cloned.1.call-start = ((), (), s32[]{:S(2)}) async-start(), calls=%async_computation.81 | async-start | bytes 1769472 | tf_op jit(solution)/shard_map/all_gather | solution.py:93
  75.5 80.8 %all-gather.12.cloned.1.call-start = ((), (), s32[]{:S(2)}) async-start(), calls=%async_computation.53 | async-start | bytes 1253376 | tf_op jit(solution)/shard_map/all_gather | solution.py:100
  77.6 115.4 %all-gather.10.cloned.1.call-start = ((), (), s32[]{:S(2)}) async-start(), calls=%async_computation.52 | async-start | bytes 1253376 | tf_op jit(solution)/shard_map/all_gather | solution.py:99
  118.0 85.5 %reduce-scatter.48.cloned.1.call-start = ((), (), s32[]{:S(2)}) async-start(), calls=%async_computation.55 | async-start | bytes 1228800 | tf_op jit(solution)/shard_map/reduce_scatter | solution.py:54
  151.9 70.5 %reduce-scatter.46.cloned.1.call-start = ((), (), s32[]{:S(2)}) async-start(), calls=%async_computation.54 | async-start | bytes 491520 | tf_op jit(solution)/shard_map/reduce_scatter | solution.py:54
  325.1 80.5 %reduce-scatter.64.cloned.1.call-start = ((), (), s32[]{:S(2)}) async-start(), calls=%async_computation.63 | async-start | bytes 1228800 | tf_op jit(solution)/shard_map/reduce_scatter | solution.py:54
  347.7 67.0 %reduce-scatter.52.cloned.1.call-start = ((), (), s32[]{:S(2)}) async-start(), calls=%async_computation.57 | async-start | bytes 1228800 | tf_op jit(solution)/shard_map/reduce_scatter | solution.py:54
  374.7 93.0 %reduce-scatter.62.cloned.1.call-start = ((), (), s32[]{:S(2)}) async-start(), calls=%async_computation.62 | async-start | bytes 491520 | tf_op jit(solution)/shard_map/reduce_scatter | solution.py:54
  476.1 64.6 %all-to-all-start.4 = ((bf16[16,40,192]{2,1,0:T(8,128)(2,1)}), bf16[16,40,192]{2,1,0:T(8,128)(2,1)}, u32[]{:S(2)}, u32[]{:S(2)}) async-start(bf16[16,40,192]{2,1,0:T(8,128)(2,1)} %multiply_convert_fusion.9), calls=%async_computation.9 | async-start | bytes 655360 | tf_op jit(solution)/shard_map/all_to_all | solution.py:60
  482.8 81.1 %reduce-scatter.86.cloned.1.call-start = ((), (), s32[]{:S(2)}) async-start(), calls=%async_computation.74 | async-start | bytes 491520 | tf_op jit(solution)/shard_map/reduce_scatter | solution.py:54
  540.6 84.6 %reduce-scatter.54.cloned.1.call-start = ((), (), s32[]{:S(2)}) async-start(), calls=%async_computation.58 | async-start | bytes 1228800 | tf_op jit(solution)/shard_map/reduce_scatter | solution.py:54
  634.2 56.9 %reduce-scatter.56.cloned.1.call-start = ((), (), s32[]{:S(2)}) async-start(), calls=%async_computation.59 | async-start | bytes 491520 | tf_op jit(solution)/shard_map/reduce_scatter | solution.py:54
  666.5 68.3 %reduce-scatter.58.cloned.1.call-start = ((), (), s32[]{:S(2)}) async-start(), calls=%async_computation.60 | async-start | bytes 491520 | tf_op jit(solution)/shard_map/reduce_scatter | solution.py:54
  761.1 97.3 %reduce-scatter.70.cloned.1.call-start = ((), (), s32[]{:S(2)}) async-start(), calls=%async_computation.66 | async-start | bytes 1228800 | tf_op jit(solution)/shard_map/reduce_scatter | solution.py:54
  885.2 64.1 %reduce-scatter.74.cloned.1.call-start = ((), (), s32[]{:S(2)}) async-start(), calls=%async_computation.68 | async-start | bytes 491520 | tf_op jit(solution)/shard_map/reduce_scatter | solution.py:54
  932.2 117.5 %reduce-scatter.78.cloned.1.call-start = ((), (), s32[]{:S(2)}) async-start(), calls=%async_computation.70 | async-start | bytes 1228800 | tf_op jit(solution)/shard_map/reduce_scatter | solution.py:54
  971.4 131.4 %reduce-scatter.80.cloned.1.call-start = ((), (), s32[]{:S(2)}) async-start(), calls=%async_computation.71 | async-start | bytes 1228800 | tf_op jit(solution)/shard_map/reduce_scatter | solution.py:54
  1005.7 141.0 %reduce-scatter.94.cloned.1.call-start = ((), (), s32[]{:S(2)}) async-start(), calls=%async_computation.78 | async-start | bytes 1253376 | tf_op jit(solution)/shard_map/reduce_scatter | solution.py:330
  1055.1 123.6 %reduce-scatter.102.cloned.1.call-start = ((), (), s32[]{:S(2)}) async-start(), calls=%async_computation.84 | async-start | bytes 1253376
  1111.8 89.3 %reduce-scatter.82.cloned.1.call-start = ((), (), s32[]{:S(2)}) async-start(), calls=%async_computation.72 | async-start | bytes 491520 | tf_op jit(solution)/shard_map/reduce_scatter | solution.py:54
  1133.7 446.1 %reduce-scatter.90.cloned.1.call-start = ((), (), s32[]{:S(2)}) async-start(), calls=%async_computation.76 | async-start | bytes 1228800 | tf_op jit(solution)/shard_map/reduce_scatter | solution.py:54
  1142.6 455.0 %reduce-scatter.100.cloned.1.call-start = ((), (), s32[]{:S(2)}) async-start(), calls=%async_computation.83 | async-start | bytes 294912
  1148.5 450.8 %reduce-scatter.96.cloned.1.call-start = ((), (), s32[]{:S(2)}) async-start(), calls=%async_computation.79 | async-start | bytes 294912 | tf_op jit(solution)/shard_map/reduce_scatter | solution.py:342
  1180.4 420.4 %reduce-scatter.106.cloned.1.call-start = ((), (), s32[]{:S(2)}) async-start(), calls=%async_computation.86 | async-start | bytes 1769472
  1188.1 415.3 %reduce-scatter.98.cloned.1.call-start = ((), (), s32[]{:S(2)}) async-start(), calls=%async_computation.80 | async-start | bytes 1769472 | tf_op jit(solution)/shard_map/reduce_scatter | solution.py:348
  1197.8 407.8 %reduce-scatter.104.cloned.1.call-start = ((), (), s32[]{:S(2)}) async-start(), calls=%async_computation.85 | async-start | bytes 294912
  1567.3 80.5 %reduce-scatter.92.cloned.1.call-start = ((), (), s32[]{:S(2)}) async-start(), calls=%async_computation.77 | async-start | bytes 417792 | tf_op jit(solution)/shard_map/reduce_scatter | solution.py:327
  1568.6 101.9 %reduce-scatter.88.cloned.1.call-start = ((), (), s32[]{:S(2)}) async-start(), calls=%async_computation.75 | async-start | bytes 491520 | tf_op jit(solution)/shard_map/reduce_scatter | solution.py:54
  1572.8 120.8 %reduce-scatter.84.cloned.1.call-start = ((), (), s32[]{:S(2)}) async-start(), calls=%async_computation.73 | async-start | bytes 491520 | tf_op jit(solution)/shard_map/reduce_scatter | solution.py:54
  1576.5 192.8 %reduce-scatter.108.cloned.1.call-start = ((), (), s32[]{:S(2)}) async-start(), calls=%async_computation.87 | async-start | bytes 1044480
  (273 other events, 8102.9 us)
Sparse Core Ops, SparseCore 0:
  74.4 18.9 reduce-scatter.43
  152.1 19.0 reduce-scatter.47
  197.5 20.0 reduce-scatter.45
  243.1 18.1 reduce-scatter.49
  264.1 20.4 reduce-scatter.59
  347.8 23.8 reduce-scatter.63
  374.8 23.9 reduce-scatter.51
  401.3 20.5 reduce-scatter.61
  528.5 20.5 reduce-scatter.85
  551.5 20.6 reduce-scatter.65
  574.5 20.5 reduce-scatter.75
  598.2 23.7 reduce-scatter.53
  656.1 16.6 reduce-scatter.55
  709.5 16.8 reduce-scatter.57
  729.3 22.9 reduce-scatter.67
  838.8 19.4 reduce-scatter.69
  885.3 16.9 reduce-scatter.71
  932.3 16.9 reduce-scatter.73
  956.2 23.6 reduce-scatter.77
  1005.8 20.9 reduce-scatter.79
  1030.6 72.2 reduce-scatter.93
  1106.1 72.5 reduce-scatter.101
  1181.1 19.9 reduce-scatter.81
  1203.6 22.7 reduce-scatter.89
  1228.7 9.9 reduce-scatter.99
  1241.0 11.5 reduce-scatter.95
  1254.8 12.7 reduce-scatter.105
  1270.6 12.7 reduce-scatter.97
  1574.0 73.8 reduce-scatter.91
  1650.4 20.0 reduce-scatter.87
  1672.9 20.6 reduce-scatter.83
  1697.0 72.3 reduce-scatter.107
  (1 shorter events, 3.4 us)
Sparse Core Ops, SparseCore 1:
  76.6 9.7 all-gather.15
  88.0 13.1 all-gather.13
  103.2 45.1 all-gather.11
  150.5 42.4 all-gather.9
where the time goes:
time: 1790 us; the launch traced here: 1780 us
  blocking collectives  797 us (45%)
  waiting for transfers between devices  373 us (21%)
  matrix products  180 us (10%)
  local copies, waits for them, and re-layouts  175 us (10%)
  other arithmetic  134 us (7%)
  starting transfers between devices  98 us (5%)
  between operations  21.1 us (1%)
    all_gather x27, blocking collectives, gather_features(): return lax.all_gather(values, 'col', axis=1, tiled=True)  371 us
    psum x1, blocking collectives, body(): small = lax.psum((totals[6], totals[7], totals[8]), ('row', 'col'))  347 us
    reduce_scatter x24, waiting for transfers between devices, sum_features(): lax.psum_scatter(values.astype(jnp.bfloat16), 'col', scatter_dimension=1,...  108 us
    unnamed x42, waiting for transfers between devices  102 us
    dot_general x33, matrix products, matmul(): return jnp.dot(left, right, preferred_element_type=jnp.float32)  86.7 us
    scatter-add x3, other arithmetic, gate_values(): return jnp.take_along_axis(jax.nn.softmax(logits, axis=-1), choices, axis=1)  65.7 us
    all_to_all x9, waiting for transfers between devices, return_rows(): lax.all_to_all(values, 'row', split_axis=0, concat_axis=0, tiled=True)  55.4 us
    all_to_all x9, starting transfers between devices, return_rows(): lax.all_to_all(values, 'row', split_axis=0, concat_axis=0, tiled=True)  51.1 us
  transfers between devices with their start and end apart: 57, of which 28 were waited for; matrix products, arithmetic and copies ran while one was open for 21% of the time, Pallas kernels for 0%

commit v1 on v0

v1 whole, which is shorter than its diff:
```python
import jax
import jax.numpy as jnp
from jax import lax
from jax.sharding import PartitionSpec as P

HD = 64
SEQ = 197
CAP = 40

exact_mode = lax.Precision.HIGHEST
BF = jnp.bfloat16
F32 = jnp.float32


def swap(block):
    return lax.ppermute(block, "section", [(0, 1), (1, 0)])


def from_col(block, distance):
    return lax.ppermute(block, "col", [(i, (i + distance) % 4) for i in range(4)])


def matmul(left, right):
    return jnp.dot(left, right, preferred_element_type=F32)


def matmul_left_t(left, right):
    return lax.dot_general(left, right, (((0,), (0,)), ((), ())), preferred_element_type=F32)


def matmul_right_t(left, right):
    return lax.dot_general(left, right, (((1,), (1,)), ((), ())), preferred_element_type=F32)


def norm_parts(values):
    centre = values - jnp.mean(values, axis=-1, keepdims=True)
    spread = jnp.mean(centre * centre, axis=-1, keepdims=True)
    inverse = lax.rsqrt(spread + 1e-06)
    return centre * inverse, inverse


def norm_back(grad, gain, normed, inverse):
    scaled = grad * gain
    return inverse * (
        scaled
        - jnp.mean(scaled, axis=-1, keepdims=True)
        - normed * jnp.mean(scaled * normed, axis=-1, keepdims=True)
    )


def cdf_of(values):
    return 0.5 * (1.0 + lax.erf(values * 0.7071067811865476))


def gelu(values):
    return (values * cdf_of(values)).astype(BF)


def gelu_slope(values):
    return cdf_of(values) + values * jnp.exp(-0.5 * values * values) * 0.3989422804014327


def two_terms(values):
    upper = lax.optimization_barrier(values.astype(BF))
    lower = (values - upper.astype(F32)).astype(BF)
    return upper, lower


def col_sum(part):
    own = lax.optimization_barrier(part.astype(BF))
    parts = [own] + [from_col(own, distance) for distance in (1, 2, 3)]
    parts = [piece.astype(F32) for piece in parts]
    return (parts[0] + parts[2]) + (parts[1] + parts[3])


def row_exchange(values):
    return lax.all_to_all(values, "row", split_axis=0, concat_axis=0, tiled=True)


def heads_of(project, kind):
    tokens, width = project.shape
    return project.reshape(tokens, width // (3 * HD), 3, HD)[:, :, kind]


def shares_of(project):
    scores = jnp.einsum(
        "qhd,khd->hqk", heads_of(project, 0), heads_of(project, 1), preferred_element_type=F32
    ) * (HD ** (-0.5))
    return jax.nn.softmax(scores, axis=-1)


def body(ends, gain_attn, w_qkv, w_out, gain_ffn, w_fc1, w_fc2, router, w_up, w_down, routes):
    tokens = ends.shape[2]
    quarter = ends.shape[3]
    width = 4 * quarter
    experts = 16
    slots = experts * CAP
    first = lax.axis_index("section") == 0
    column = lax.axis_index("col")
    expert = lax.axis_index("row")

    packed = jnp.concatenate(
        [w_fc1, w_fc2.T, w_out[0].T, jnp.zeros((48, 64), BF), w_qkv[0]], axis=1
    )
    gathered = lax.all_gather(packed, ("section", "col", "row"), axis=0, tiled=True)
    gathered = gathered.reshape(2, 4, width, packed.shape[1])
    fc_in = gathered[:, :, :, :384].reshape(8, width, 384)
    fc_out_t = gathered[:, :, :, 384:768].reshape(8, width, 384)
    out_t = gathered[:, :, :, 768 : 768 + quarter]
    qkv = gathered[:, :, :, 1024:]

    kept = jnp.where(first, ends[0, 0], ends[0, 1])
    other = swap(jnp.where(first, ends[0, 1], ends[0, 0]))
    start = lax.all_gather(jnp.where(first, kept, other), "col", axis=1, tiled=True)
    cotangent = lax.all_gather(jnp.where(first, other, kept), "col", axis=1, tiled=True)
    choices = jnp.where(first, routes[0], routes[1])
    gains = [swap(gain_attn), swap(gain_ffn)]
    gain_one = [
        jnp.where(first, gain_attn[0], gains[0][0]),
        jnp.where(first, gains[0][0], gain_attn[0]),
    ]
    gain_two = [
        jnp.where(first, gain_ffn[0], gains[1][0]),
        jnp.where(first, gains[1][0], gain_ffn[0]),
    ]
    router_other = swap(router)
    gate_table = jnp.concatenate(
        [jnp.where(first, router, router_other), jnp.where(first, router_other, router)], axis=0
    )
    up_other = swap(w_up[0])
    down_other = swap(w_down[0])
    up_block = jnp.concatenate(
        [jnp.where(first, w_up[0], up_other), jnp.where(first, up_other, w_up[0])], axis=0
    )
    down_block = jnp.concatenate(
        [jnp.where(first, w_down[0], down_other), jnp.where(first, down_other, w_down[0])], axis=1
    )

    kinds = jnp.arange(experts, dtype=jnp.int32)
    hot = [(choices[:, i : i + 1] == kinds[None, :]).astype(F32) for i in range(2)]
    order = jnp.arange(tokens, dtype=jnp.int32)
    before = (order[None, :] < order[:, None]).astype(BF)
    counts = matmul(before, (hot[0] + hot[1]).astype(BF))
    places = jnp.arange(slots, dtype=jnp.int32)
    taken = []
    for i in range(2):
        target = choices[:, i] * CAP + jnp.sum(counts * hot[i], axis=1).astype(jnp.int32)
        taken.append((target[:, None] == places[None, :]).astype(BF))
    both = taken[0] + taken[1]

    grad_slots = matmul_left_t(both, cotangent).astype(BF)
    grad_slots = row_exchange(grad_slots.reshape(experts, CAP, width)).reshape(slots, width)

    def attend(values, layer):
        normed, inverse = norm_parts(values)
        attn_in = (normed * gain_one[layer]).astype(BF)
        project = jnp.concatenate(
            [matmul(attn_in, qkv[layer, k]).astype(BF) for k in range(4)], axis=1
        )
        shares = shares_of(project)
        mixed = jnp.einsum(
            "hqk,khd->qhd", shares.astype(BF), heads_of(project, 2), preferred_element_type=F32
        )
        mixed = mixed.astype(BF).reshape(tokens, width)
        middle = values + sum(
            matmul_right_t(mixed[:, k * quarter : (k + 1) * quarter], out_t[layer, k])
            for k in range(4)
        )
        normed_two, inverse_two = norm_parts(middle.astype(BF).astype(F32))
        second = (normed_two * gain_two[layer]).astype(BF)
        kept = (normed, inverse, attn_in, project, shares, mixed, normed_two, inverse_two)
        return middle, second, kept

    def attend_back(kept, layer, grad_out, grad_second):
        normed, inverse, attn_in, project, shares, mixed, normed_two, inverse_two = kept
        grad_gain_two = jnp.sum(grad_second * normed_two, axis=0)
        grad_middle = grad_out + norm_back(grad_second, gain_two[layer], normed_two, inverse_two)
        branch = grad_middle.astype(BF)
        mine = lax.dynamic_slice_in_dim(mixed, column * quarter, quarter, 1)
        grad_out_t = matmul_left_t(branch, mine)
        grad_mixed = jnp.concatenate(
            [matmul(branch, out_t[layer, k]).astype(BF) for k in range(4)], axis=1
        ).reshape(tokens, -1, HD)
        grad_shares = jnp.einsum(
            "qhd,khd->hqk", grad_mixed, heads_of(project, 2), preferred_element_type=F32
        )
        grad_values = jnp.einsum(
            "hqk,qhd->khd", shares.astype(BF), grad_mixed, preferred_element_type=F32
        )
        grad_scores = shares * (
            grad_shares - jnp.sum(grad_shares * shares, axis=-1, keepdims=True)
        )
        grad_scores = grad_scores.astype(BF)
        scale = HD ** (-0.5)
        grad_queries = scale * jnp.einsum(
            "hqk,khd->qhd", grad_scores, heads_of(project, 1), preferred_element_type=F32
        )
        grad_keys = scale * jnp.einsum(
            "hqk,qhd->khd", grad_scores, heads_of(project, 0), preferred_element_type=F32
        )
        grad_project = jnp.stack([grad_queries, grad_keys, grad_values], axis=2).astype(BF)
        grad_project = grad_project.reshape(tokens, -1)
        third = 3 * quarter
        mine = lax.dynamic_slice_in_dim(grad_project, column * third, third, 1)
        grad_qkv = matmul_left_t(attn_in, mine)
        grad_in = sum(
            matmul_right_t(grad_project[:, k * third : (k + 1) * third], qkv[layer, k])
            for k in range(4)
        )
        grad_gain_one = jnp.sum(grad_in * normed, axis=0)
        grad_values_in = grad_middle + norm_back(grad_in, gain_one[layer], normed, inverse)
        return grad_values_in, grad_qkv, grad_out_t, grad_gain_one, grad_gain_two

    middle, second, kept_first = attend(start.astype(F32), 0)
    second_first = second
    hidden = jnp.einsum("td,kdh->kth", second, fc_in, preferred_element_type=F32)
    active = gelu(hidden)
    dense = jnp.einsum("kth,kdh->td", active, fc_out_t, preferred_element_type=F32)
    handed = (middle + dense).astype(BF)

    middle, second, kept_second = attend(handed.astype(F32), 1)
    sent = matmul_left_t(both, second).astype(BF)
    rows = row_exchange(sent.reshape(experts, CAP, width)).reshape(slots, width)
    shares = jax.nn.softmax(matmul(second, gate_table), axis=-1)
    gates = [jnp.sum(shares * hot[i], axis=1) for i in range(2)]

    row_shares = jax.nn.softmax(matmul(rows, gate_table), axis=-1)
    row_gate = jnp.sum(jnp.where(kinds[None, :] == expert, row_shares, 0.0), axis=1)
    expert_hidden = matmul(rows, up_block)
    expert_active = gelu(expert_hidden)
    expert_result = matmul(expert_active, down_block)
    grad_result = (grad_slots.astype(F32) * row_gate[:, None]).astype(BF)
    grad_hidden = (matmul_right_t(grad_result, down_block) * gelu_slope(expert_hidden)).astype(BF)
    grad_rows = matmul_right_t(grad_hidden, up_block).astype(BF)
    grad_gate_slots = jnp.sum(grad_slots.astype(F32) * expert_result, axis=1)
    upper, lower = two_terms(grad_gate_slots.reshape(experts, 1, CAP))
    tail = jnp.pad(jnp.concatenate([upper, lower], axis=1), ((0, 0), (0, 6), (0, width - CAP)))
    returned = row_exchange(
        jnp.concatenate([grad_rows.reshape(experts, CAP, width), tail], axis=1)
    )
    grad_down = matmul_left_t(expert_active, grad_result)
    grad_up = matmul_left_t(rows, grad_hidden)
    result_back = row_exchange(expert_result.astype(BF).reshape(experts, CAP, width))
    result_back = result_back.reshape(slots, width)

    gate_slots = returned[:, CAP, :CAP].astype(F32) + returned[:, CAP + 1, :CAP].astype(F32)
    gate_slots = gate_slots.reshape(1, slots)
    gate_parts = jnp.stack(
        [jnp.sum(taken[i].astype(F32) * gate_slots, axis=1) for i in range(2)], axis=0
    )
    upper, lower = two_terms(gate_parts)
    tail = jnp.pad(jnp.concatenate([upper, lower], axis=0), ((0, 7), (0, width - tokens)))
    part = matmul(both, returned[:, :CAP].reshape(slots, width)).astype(BF)
    summed = col_sum(jnp.concatenate([part, tail], axis=0))
    grad_gates = [summed[tokens + i, :tokens] + summed[tokens + 2 + i, :tokens] for i in range(2)]
    weighted = grad_gates[0] * gates[0] + grad_gates[1] * gates[1]
    grad_logits = shares * (
        hot[0] * grad_gates[0][:, None] + hot[1] * grad_gates[1][:, None] - weighted[:, None]
    )
    grad_router = jnp.dot(second.astype(F32).T, grad_logits, precision=exact_mode)
    grad_second = summed[:tokens] + jnp.dot(
        grad_logits, gate_table.astype(F32).T, precision=exact_mode
    )
    grad_in, grad_qkv_b, grad_out_b, grad_gain_one_b, grad_gain_two_b = attend_back(
        kept_second, 1, cotangent.astype(F32), grad_second
    )

    picked = gates[0][:, None] * matmul(taken[0], result_back) + gates[1][:, None] * matmul(
        taken[1], result_back
    )
    picked = picked.astype(BF).reshape(tokens, 4, quarter).transpose(1, 0, 2)
    picked = lax.all_to_all(picked, "col", split_axis=0, concat_axis=0, tiled=True)
    result = lax.dynamic_slice_in_dim(middle, column * quarter, quarter, 1) + jnp.sum(
        picked.astype(F32), axis=0
    )
    result = result.astype(BF)

    grad_dense = grad_in.astype(BF)
    grad_hidden = jnp.einsum("td,kdh->kth", grad_dense, fc_out_t, preferred_element_type=F32)
    grad_hidden = (grad_hidden * gelu_slope(hidden)).astype(BF)
    grad_second = jnp.einsum("kth,kdh->td", grad_hidden, fc_in, preferred_element_type=F32)

    def own_blocks(values):
        return [
            lax.dynamic_index_in_dim(values, column + 4 * k, 0, keepdims=False) for k in range(2)
        ]

    grad_fc_in = [matmul_left_t(second_first, block) for block in own_blocks(grad_hidden)]
    grad_fc_out_t = [matmul_left_t(grad_dense, block) for block in own_blocks(active)]
    grad_in, grad_qkv_a, grad_out_a, grad_gain_one_a, grad_gain_two_a = attend_back(
        kept_first, 0, grad_in, grad_second
    )
    grad_start = lax.dynamic_slice_in_dim(grad_in, column * quarter, quarter, 1).astype(BF)

    given = swap(jnp.where(first, result, grad_start))
    ends_out = jnp.stack(
        [jnp.where(first, grad_start, given), jnp.where(first, given, result)]
    )[None]

    def both_sections(for_first, for_second):
        ours = jnp.where(first, for_first, for_second)
        theirs = swap(jnp.where(first, for_second, for_first).astype(BF))
        return ours + theirs.astype(F32)

    def over_rows(total):
        pieces = row_exchange(total.astype(BF).reshape(16, 48, total.shape[1]))
        return jnp.sum(pieces.astype(F32), axis=0)

    sum_fc = both_sections(
        jnp.concatenate([grad_fc_in[0], grad_fc_out_t[0]], axis=1),
        jnp.concatenate([grad_fc_in[1], grad_fc_out_t[1]], axis=1),
    )
    shard_fc = over_rows(sum_fc)
    sum_attn = both_sections(
        jnp.concatenate([grad_out_a, grad_qkv_a], axis=1),
        jnp.concatenate([grad_out_b, grad_qkv_b], axis=1),
    )
    shard_attn = over_rows(sum_attn)
    small = both_sections(
        jnp.concatenate(
            [grad_gain_one_a, grad_gain_two_a, grad_router[: width // 2].reshape(-1)]
        ),
        jnp.concatenate(
            [grad_gain_one_b, grad_gain_two_b, grad_router[width // 2 :].reshape(-1)]
        ),
    )
    upper, lower = two_terms(small)
    small = jnp.concatenate([upper, lower]).reshape(1, -1, 128)
    small = row_exchange(jnp.broadcast_to(small, (16,) + small.shape[1:]))
    small = jnp.sum(small.astype(F32), axis=0).reshape(2, -1)
    small = small[0] + small[1]
    sum_up = both_sections(grad_up[: width // 2], grad_up[width // 2 :])
    sum_down = both_sections(grad_down[:, : width // 2], grad_down[:, width // 2 :])
    return (
        ends_out,
        small[None, :width],
        shard_attn[None, :, quarter:],
        shard_attn[:, :quarter].T[None],
        small[None, width : 2 * width],
        shard_fc[:, :384],
        shard_fc[:, 384:].T,
        small[2 * width :].reshape(width // 2, experts),
        sum_up[None],
        sum_down[None],
    )


def solution(mesh):
    placed = (
        P("section", None, "row", "col"),
        P("section", None),
        P("section", "row", "col"),
        P("section", "col", "row"),
        P("section", None),
        P("row", ("section", "col")),
        P(("section", "col"), "row"),
        P("section", None),
        P("row", "section", "col"),
        P("row", "col", "section"),
        P(None, "row", None),
    )
    return jax.shard_map(
        body,
        mesh=mesh,
        in_specs=placed,
        out_specs=(
            P("section", None, "row", "col"),
            P("section", None),
            P("section", "row", "col"),
            P("section", "col", "row"),
            P("section", None),
            P("row", ("section", "col")),
            P(("section", "col"), "row"),
            P("section", None),
            P("row", "section", "col"),
            P("row", "col", "section"),
        ),
        check_vma=False,
    )
```

time: 1790 us -> 434 us (0.24)
  blocking collectives: 797 us -> 26.6 us
  waiting for transfers between devices: 373 us -> 118 us
  local copies, waits for them, and re-layouts: 175 us -> 53.8 us
  other arithmetic: 134 us -> 46.7 us
  matrix products: 180 us -> 116 us
  starting transfers between devices: 98 us -> 48 us
    all_gather x32 -> x2, blocking collectives: 426 us -> 26.6 us  [the longest x1 13.6 us: body(): lax.all_gather(jnp.where(first, other, kept), 'col', axis=1, tiled=True)]
    psum x1 -> x0, blocking collectives: 347 us -> none  [body(): small = lax.psum((totals[6], totals[7], totals[8]), ('row', 'col'))]
    reduce_scatter x28 -> x0, waiting for transfers between devices: 148 us -> none  [the longest x24 108 us: sum_features(): lax.psum_scatter(values.astype(jnp.bfloat16), 'col', scatter_dimension=1,...]
    unnamed x42 -> x1, waiting for transfers between devices: 102 us -> 0.02 us
    gather x33 -> x0, local copies, waits for them, and re-layouts: 81.6 us -> none  [the longest x15 37 us: gate_values(): return jnp.take_along_axis(jax.nn.softmax(logits, axis=-1), choices, axis=1)]
    scatter-add x3 -> x0, other arithmetic: 65.7 us -> none  [gate_values(): return jnp.take_along_axis(jax.nn.softmax(logits, axis=-1), choices, axis=1)]
    all_to_all x16 -> x8, starting transfers between devices: 89.3 us -> 40 us  [the longest x7 35.9 us: row_exchange(): lax.all_to_all(values, 'row', split_axis=0, concat_axis=0, tiled=True)]
    all_to_all x16 -> x8, waiting for transfers between devices: 85.8 us -> 40 us  [the longest x7 40 us: row_exchange(): lax.all_to_all(values, 'row', split_axis=0, concat_axis=0, tiled=True)]
  transfers between devices with their start and end apart: 57 -> 24, of which waited for: 28 -> 10; matrix products, arithmetic and copies ran while one was open for 21% -> 48% of each run, Pallas kernels for 0% -> 0%
where the time goes in v1:
time: 434 us; the launch traced here: 426 us
  waiting for transfers between devices  118 us (27%)
  matrix products  116 us (27%)
  local copies, waits for them, and re-layouts  53.8 us (12%)
  starting transfers between devices  48 us (11%)
  other arithmetic  46.7 us (11%)
  blocking collectives  26.6 us (6%)
  between operations  16.1 us (4%)
    all_gather x1, waiting for transfers between devices, body(): lax.all_gather(packed, ('section', 'col', 'row'), axis=0, tiled=True)  71.3 us
    dot_general x24, matrix products, matmul(): return jnp.dot(left, right, preferred_element_type=F32)  41.2 us
    all_to_all x7, waiting for transfers between devices, row_exchange(): lax.all_to_all(values, 'row', split_axis=0, concat_axis=0, tiled=True)  40 us
    all_to_all x7, starting transfers between devices, row_exchange(): lax.all_to_all(values, 'row', split_axis=0, concat_axis=0, tiled=True)  35.9 us
    dot_general x18, matrix products, matmul_right_t(): lax.dot_general(left, right, (((1,), (1,)), ((), ())), preferred_element_...  33.9 us
    dot_general x12, matrix products, matmul_left_t(): lax.dot_general(left, right, (((0,), (0,)), ((), ())), preferred_element_...  20.5 us
    all_gather x1, blocking collectives, body(): lax.all_gather(jnp.where(first, other, kept), 'col', axis=1, tiled=True)  13.6 us
    all_gather x1, blocking collectives, body(): lax.all_gather(jnp.where(first, kept, other), 'col', axis=1, tiled=True)  13 us
  transfers between devices with their start and end apart: 24, of which 10 were waited for; matrix products, arithmetic and copies ran while one was open for 48% of the time, Pallas kernels for 0%

profile of v1, /device:TPU:0, one launch (start us, length us, event | category | flops | bytes accessed | tf_op | source)
XLA Modules:
  0.0 425.8 jit_solution(17505045978376769071)
XLA Ops:
  15.0 13.0 %all_gather.10 = bf16[197,768]{0,1:T(8,128)(2,1)S(1)} all-gather(bf16[197,192]{0,1:T(8,128)(2,1)S(1)} %copy.131), channel_id=1, replica_groups=mesh['section'=2,'row'=16,'col'=4] {'col'}, dimensions={1}, use_global_device_ids=true | all-gather | bytes 378240 | tf_op jit(solution)/shard_map/all_gather | solution.py:114
  28.6 71.3 %all-gather.2.cloned.1.call-done = bf16[6144,1600]{1,0:T(8,128)(2,1)} async-done(((bf16[48,1600]{1,0:T(8,128)(2,1)}), bf16[6144,1600]{1,0:T(8,128)(2,1)}) %all-gather.2.cloned.1.call-update) | async-done | bytes 19660816 | tf_op jit(solution)/shard_map/all_gather | solution.py:105
  106.7 8.6 %fusion.220 = (bf16[2,4,768,384]{3,2,1,0:T(8,128)(2,1)}, bf16[2,4,768,384]{3,2,1,0:T(8,128)(2,1)}) fusion(bf16[2,4,768,1600]{3,2,1,0:T(8,128)(2,1)} %bitcast.323), kind=kLoop, calls=%fused_computation.419 | loop fusion | bytes 18874368 | tf_op jit(solution)/shard_map/slice | solution.py:108
  128.6 3.1 fusion.11
  162.4 6.5 %all-to-all-start.1 = ((bf16[16,40,768]{2,1,0:T(8,128)(2,1)}), bf16[16,40,768]{2,1,0:T(8,128)(2,1)}, u32[]{:S(2)}, u32[]{:S(2)}) async-start(bf16[16,40,768]{2,1,0:T(8,128)(2,1)} %bitcast.387), calls=%async_computation.1 | async-start | bytes 1966080 | tf_op jit(solution)/shard_map/all_to_all | solution.py:77
  170.3 13.6 %all_gather.9 = bf16[197,768]{0,1:T(8,128)(2,1)} all-gather(bf16[197,192]{0,1:T(8,128)(2,1)} %copy.129), channel_id=1, replica_groups=mesh['section'=2,'row'=16,'col'=4] {'col'}, dimensions={1}, use_global_device_ids=true | all-gather | bytes 378240 | tf_op jit(solution)/shard_map/all_gather | solution.py:115
  189.9 7.5 %all-to-all-start = ((bf16[16,40,768]{2,1,0:T(8,128)(2,1)}), bf16[16,40,768]{2,1,0:T(8,128)(2,1)}, u32[]{:S(2)}, u32[]{:S(2)}) async-start(bf16[16,40,768]{2,1,0:T(8,128)(2,1)} %bitcast.384), calls=%async_computation | async-start | bytes 1966080 | tf_op jit(solution)/shard_map/all_to_all | solution.py:77
  201.0 3.7 multiply_convert_fusion.2
  204.6 8.1 %all-to-all-done = bf16[16,40,768]{2,1,0:T(8,128)(2,1)} async-done(((bf16[16,40,768]{2,1,0:T(8,128)(2,1)}), bf16[16,40,768]{2,1,0:T(8,128)(2,1)}, u32[]{:S(2)}, u32[]{:S(2)}) %all-to-all-start) | async-done | bytes 983072 | tf_op jit(solution)/shard_map/all_to_all | solution.py:77
  212.7 4.1 fusion.221
  217.0 4.3 %all-to-all-start.3 = ((bf16[16,40,768]{2,1,0:T(8,128)(2,1)}), bf16[16,40,768]{2,1,0:T(8,128)(2,1)}, u32[]{:S(2)}, u32[]{:S(2)}) async-start(bf16[16,40,768]{2,1,0:T(8,128)(2,1)} %bitcast.388), calls=%async_computation.3 | async-start | bytes 1966080 | tf_op jit(solution)/shard_map/all_to_all | solution.py:77
  221.3 3.5 fusion.25
  231.7 3.9 all-to-all-done.3
  235.6 4.4 %all-to-all-start.2 = ((bf16[16,48,768]{2,1,0:T(8,128)(2,1)}), bf16[16,48,768]{2,1,0:T(8,128)(2,1)}, u32[]{:S(2)}, u32[]{:S(2)}) async-start(bf16[16,48,768]{2,1,0:T(8,128)(2,1)} %pad_maximum_fusion.6), calls=%async_computation.2 | async-start | bytes 2359296 | tf_op jit(solution)/shard_map/all_to_all | solution.py:77
  240.0 2.6 fusion.231
  253.2 5.5 %all-to-all-done.2 = bf16[16,48,768]{2,1,0:T(8,128)(2,1)} async-done(((bf16[16,48,768]{2,1,0:T(8,128)(2,1)}), bf16[16,48,768]{2,1,0:T(8,128)(2,1)}, u32[]{:S(2)}, u32[]{:S(2)}) %all-to-all-start.2) | async-done | bytes 1179680 | tf_op jit(solution)/shard_map/all_to_all | solution.py:77
  258.7 4.1 all-to-all-start.4
  266.8 3.2 collective-permute-start.8
  270.0 2.8 collective-permute-start.6
  278.6 3.6 collective-permute-done.8
  331.9 3.1 fusion.45
  342.6 3.8 select_convert_fusion
  351.8 3.4 fusion.214
  357.3 5.0 %all-to-all-start.5 = ((bf16[16,120,128]{2,1,0:T(8,128)(2,1)}), bf16[16,120,128]{2,1,0:T(8,128)(2,1)}, u32[]{:S(2)}, u32[]{:S(2)}) async-start(bf16[16,120,128]{2,1,0:T(8,128)(2,1)} %broadcast_in_dim.30), calls=%async_computation.5 | async-start | bytes 983040 | tf_op jit(solution)/shard_map/all_to_all | solution.py:77
  363.1 3.0 add_convert_fusion.1
  368.5 5.4 %all-to-all-done.5 = bf16[16,120,128]{2,1,0:T(8,128)(2,1)} async-done(((bf16[16,120,128]{2,1,0:T(8,128)(2,1)}), bf16[16,120,128]{2,1,0:T(8,128)(2,1)}, u32[]{:S(2)}, u32[]{:S(2)}) %all-to-all-start.5) | async-done | bytes 491552 | tf_op jit(solution)/shard_map/all_to_all | solution.py:77
  373.9 4.4 %all-to-all-start.6 = ((bf16[16,48,768]{2,1,0:T(8,128)(2,1)}), bf16[16,48,768]{2,1,0:T(8,128)(2,1)}, u32[]{:S(2)}, u32[]{:S(2)}) async-start(bf16[16,48,768]{2,1,0:T(8,128)(2,1)} %bitcast.89), calls=%async_computation.6 | async-start | bytes 2359296 | tf_op jit(solution)/shard_map/all_to_all | solution.py:77
  380.1 3.1 add_bitcast_fusion
  385.8 3.1 add_convert_fusion
  391.3 5.3 %all-to-all-done.6 = bf16[16,48,768]{2,1,0:T(8,128)(2,1)} async-done(((bf16[16,48,768]{2,1,0:T(8,128)(2,1)}), bf16[16,48,768]{2,1,0:T(8,128)(2,1)}, u32[]{:S(2)}, u32[]{:S(2)}) %all-to-all-start.6) | async-done | bytes 1179680 | tf_op jit(solution)/shard_map/all_to_all | solution.py:77
  396.5 3.7 all-to-all-start.7
  406.2 11.7 %all-to-all-done.7 = bf16[16,48,768]{2,1,0:T(8,128)(2,1)S(1)} async-done(((bf16[16,48,768]{2,1,0:T(8,128)(2,1)}), bf16[16,48,768]{2,1,0:T(8,128)(2,1)S(1)}, u32[]{:S(2)}, u32[]{:S(2)}) %all-to-all-start.7) | async-done | bytes 1179680 | tf_op jit(solution)/shard_map/all_to_all | solution.py:77
  (395 shorter events, 177.2 us)
Async XLA Ops:
  7.2 92.7 %all-gather.2.cloned.1.call-start = ((), (), s32[]{:S(2)}) async-start(), calls=%async_computation.8 | async-start | bytes 20606976 | tf_op jit(solution)/shard_map/all_gather | solution.py:105
  8.9 3.8 collective-permute-start.1
  9.0 4.4 %collective-permute-start.2 = (f32[1,768]{1,0:T(1,128)}, f32[1,768]{1,0:T(1,128)S(1)}, u32[]{:S(2)}, u32[]{:S(2)}) collective-permute-start(f32[1,768]{1,0:T(1,128)} %param.15), channel_id=1, source_target_pairs={{0,64},{64,0},{1,65},{65,1},{2,66},{66,2},{3,67},{67,3},{4,68},{68... | collective-permute-start | bytes 9224 | tf_op jit(solution)/shard_map/ppermute | solution.py:16
  9.5 4.7 %collective-permute-start.3 = (bf16[384,16]{0,1:T(8,128)(2,1)}, bf16[384,16]{0,1:T(8,128)(2,1)S(1)}, u32[]{:S(2)}, u32[]{:S(2)}) collective-permute-start(bf16[384,16]{0,1:T(8,128)(2,1)} %param.18), channel_id=1, source_target_pairs={{0,64},{64,0},{1,65},{65,1},{2,66},{66,2},{3,67},{67,3},{4,68},{68... | collective-permute-start | bytes 36872 | tf_op jit(solution)/shard_map/ppermute | solution.py:16
  10.8 4.1 collective-permute-start
  11.3 174.5 %collective-permute-start.4 = (bf16[768,384]{1,0:T(8,128)(2,1)}, bf16[768,384]{1,0:T(8,128)(2,1)}, u32[]{:S(2)}, u32[]{:S(2)}) collective-permute-start(bf16[768,384]{1,0:T(8,128)(2,1)} %bitcast.400), channel_id=1, source_target_pairs={{0,64},{64,0},{1,65},{65,1},{2,66},{66,2},{3,67},{67,3},{4,68},{68... | collective-permute-start | bytes 1769480 | tf_op jit(solution)/shard_map/ppermute | solution.py:16
  13.4 91.6 %copy-start.38 = (f32[768]{0:T(1024)}, f32[768]{0:T(1024)S(1)}, u32[]{:S(2)}) copy-start(f32[768]{0:T(1024)S(1)} %get-tuple-element.79) | copy-start | bytes 9220
  13.4 120.3 %copy-start.40 = (f32[768]{0:T(1024)}, f32[768]{0:T(1024)S(1)}, u32[]{:S(2)}) copy-start(f32[768]{0:T(1024)S(1)} %get-tuple-element.78) | copy-start | bytes 9220
  14.1 114.4 %copy-start.36 = (f32[768]{0:T(1024)}, f32[768]{0:T(1024)S(1)}, u32[]{:S(2)}) copy-start(f32[768]{0:T(1024)S(1)} %get-tuple-element.77) | copy-start | bytes 9220
  14.1 145.1 %copy-start.42 = (f32[768]{0:T(1024)}, f32[768]{0:T(1024)S(1)}, u32[]{:S(2)}) copy-start(f32[768]{0:T(1024)S(1)} %get-tuple-element.76) | copy-start | bytes 9220
  28.1 98.5 %copy-start = (bf16[197,768]{1,0:T(8,128)(2,1)}, bf16[197,768]{1,0:T(8,128)(2,1)S(1)}, u32[]{:S(2)}) copy-start(bf16[197,768]{1,0:T(8,128)(2,1)S(1)} %copy.132) | copy-start | bytes 907780
  28.3 76.7 %copy-start.53 = (f32[197]{0:T(256)}, f32[197]{0:T(256)S(1)}, u32[]{:S(2)}) copy-start(f32[197]{0:T(256)S(1)} %broadcast_multiply_fusion.12) | copy-start | bytes 2368
  28.5 76.4 %copy-start.57 = (f32[197]{0:T(256)}, f32[197]{0:T(256)S(1)}, u32[]{:S(2)}) copy-start(f32[197]{0:T(256)S(1)} %add_rsqrt_fusion.3) | copy-start | bytes 2368
  162.4 27.4 %all-to-all-start.1 = ((bf16[16,40,768]{2,1,0:T(8,128)(2,1)}), bf16[16,40,768]{2,1,0:T(8,128)(2,1)}, u32[]{:S(2)}, u32[]{:S(2)}) async-start(bf16[16,40,768]{2,1,0:T(8,128)(2,1)} %bitcast.387), calls=%async_computation.1 | async-start | bytes 1966080 | tf_op jit(solution)/shard_map/all_to_all | solution.py:77
  168.9 28.5 %collective-permute-start.5 = (bf16[384,768]{1,0:T(8,128)(2,1)}, bf16[384,768]{1,0:T(8,128)(2,1)}, u32[]{:S(2)}, u32[]{:S(2)}) collective-permute-start(bf16[384,768]{1,0:T(8,128)(2,1)} %bitcast.401), channel_id=1, source_target_pairs={{0,64},{64,0},{1,65},{65,1},{2,66},{66,2},{3,67},{67,3},{4,68},{68... | collective-permute-start | bytes 1769480 | tf_op jit(solution)/shard_map/ppermute | solution.py:16
  170.3 18.0 %copy-start.64 = (s32[197,1]{0,1:T(1,128)S(1)}, s32[197,1]{0,1:T(1,128)}, u32[]{:S(2)}) copy-start(s32[197,1]{0,1:T(1,128)} %copy-done.63) | copy-start | bytes 2368
  189.9 22.8 %all-to-all-start = ((bf16[16,40,768]{2,1,0:T(8,128)(2,1)}), bf16[16,40,768]{2,1,0:T(8,128)(2,1)}, u32[]{:S(2)}, u32[]{:S(2)}) async-start(bf16[16,40,768]{2,1,0:T(8,128)(2,1)} %bitcast.384), calls=%async_computation | async-start | bytes 1966080 | tf_op jit(solution)/shard_map/all_to_all | solution.py:77
  217.0 18.7 %all-to-all-start.3 = ((bf16[16,40,768]{2,1,0:T(8,128)(2,1)}), bf16[16,40,768]{2,1,0:T(8,128)(2,1)}, u32[]{:S(2)}, u32[]{:S(2)}) async-start(bf16[16,40,768]{2,1,0:T(8,128)(2,1)} %bitcast.388), calls=%async_computation.3 | async-start | bytes 1966080 | tf_op jit(solution)/shard_map/all_to_all | solution.py:77
  229.5 43.3 %collective-permute-start.13 = (bf16[384,768]{1,0:T(8,128)(2,1)}, bf16[384,768]{1,0:T(8,128)(2,1)}, u32[]{:S(2)}, u32[]{:S(2)}) collective-permute-start(bf16[384,768]{1,0:T(8,128)(2,1)} %select_convert_fusion.3), channel_id=1, source_target_pairs={{0,64},{64,0},{1,65},{65,1},{2,66},{66,2},{3,67},{67,3},{4,68},{68... | collective-permute-start | bytes 1769480 | tf_op jit(solution)/shard_map/ppermute | solution.py:16
  235.6 23.1 %all-to-all-start.2 = ((bf16[16,48,768]{2,1,0:T(8,128)(2,1)}), bf16[16,48,768]{2,1,0:T(8,128)(2,1)}, u32[]{:S(2)}, u32[]{:S(2)}) async-start(bf16[16,48,768]{2,1,0:T(8,128)(2,1)} %pad_maximum_fusion.6), calls=%async_computation.2 | async-start | bytes 2359296 | tf_op jit(solution)/shard_map/all_to_all | solution.py:77
  245.0 135.1 %collective-permute-start.14 = (bf16[768,384]{1,0:T(8,128)(2,1)}, bf16[768,384]{1,0:T(8,128)(2,1)}, u32[]{:S(2)}, u32[]{:S(2)}) collective-permute-start(bf16[768,384]{1,0:T(8,128)(2,1)} %select_convert_fusion.2), channel_id=1, source_target_pairs={{0,64},{64,0},{1,65},{65,1},{2,66},{66,2},{3,67},{67,3},{4,68},{68... | collective-permute-start | bytes 1769480 | tf_op jit(solution)/shard_map/ppermute | solution.py:16
  258.7 16.4 %all-to-all-start.4 = ((bf16[4,197,192]{1,2,0:T(8,128)(2,1)}), bf16[4,197,192]{1,2,0:T(8,128)(2,1)}, u32[]{:S(2)}, u32[]{:S(2)}) async-start(bf16[4,197,192]{1,2,0:T(8,128)(2,1)} %copy.151), calls=%async_computation.4 | async-start | bytes 786432 | tf_op jit(solution)/shard_map/all_to_all | solution.py:272
  266.8 15.4 %collective-permute-start.8 = (bf16[208,768]{1,0:T(8,128)(2,1)}, bf16[208,768]{1,0:T(8,128)(2,1)}, u32[]{:S(2)}, u32[]{:S(2)}) collective-permute-start(bf16[208,768]{1,0:T(8,128)(2,1)} %pad_maximum_fusion.15), channel_id=1, source_target_pairs={{0,3},{1,0},{2,1},{3,2},{4,7},{5,4},{6,5},{7,6},{8,11},{9,8},{10,9... | collective-permute-start | bytes 958472 | tf_op jit(solution)/shard_map/ppermute | solution.py:20
  270.0 14.6 %collective-permute-start.7 = (bf16[208,768]{1,0:T(8,128)(2,1)}, bf16[208,768]{1,0:T(8,128)(2,1)}, u32[]{:S(2)}, u32[]{:S(2)}) collective-permute-start(bf16[208,768]{1,0:T(8,128)(2,1)} %pad_maximum_fusion.15), channel_id=1, source_target_pairs={{0,1},{1,2},{2,3},{3,0},{4,5},{5,6},{6,7},{7,4},{8,9},{9,10},{10,1... | collective-permute-start | bytes 958472 | tf_op jit(solution)/shard_map/ppermute | solution.py:20
  270.0 14.6 %collective-permute-start.6 = (bf16[208,768]{1,0:T(8,128)(2,1)}, bf16[208,768]{1,0:T(8,128)(2,1)}, u32[]{:S(2)}, u32[]{:S(2)}) collective-permute-start(bf16[208,768]{1,0:T(8,128)(2,1)} %pad_maximum_fusion.15), channel_id=1, source_target_pairs={{0,2},{1,3},{2,0},{3,1},{4,6},{5,7},{6,4},{7,5},{8,10},{9,11},{10,... | collective-permute-start | bytes 958472 | tf_op jit(solution)/shard_map/ppermute | solution.py:20
  346.4 39.4 %collective-permute-start.12 = (bf16[768,768]{0,1:T(8,128)(2,1)}, bf16[768,768]{0,1:T(8,128)(2,1)}, u32[]{:S(2)}, u32[]{:S(2)}) collective-permute-start(bf16[768,768]{0,1:T(8,128)(2,1)} %select_convert_fusion), channel_id=1, source_target_pairs={{0,64},{64,0},{1,65},{65,1},{2,66},{66,2},{3,67},{67,3},{4,68},{68... | collective-permute-start | bytes 3538952 | tf_op jit(solution)/shard_map/ppermute | solution.py:16
  351.4 11.7 %collective-permute-start.11 = (bf16[768,768]{0,1:T(8,128)(2,1)}, bf16[768,768]{0,1:T(8,128)(2,1)}, u32[]{:S(2)}, u32[]{:S(2)}) collective-permute-start(bf16[768,768]{0,1:T(8,128)(2,1)} %select_convert_fusion.1), channel_id=1, source_target_pairs={{0,64},{64,0},{1,65},{65,1},{2,66},{66,2},{3,67},{67,3},{4,68},{68... | collective-permute-start | bytes 3538952 | tf_op jit(solution)/shard_map/ppermute | solution.py:16
  355.2 1.3 collective-permute-start.10
  357.3 16.6 %all-to-all-start.5 = ((bf16[16,120,128]{2,1,0:T(8,128)(2,1)}), bf16[16,120,128]{2,1,0:T(8,128)(2,1)}, u32[]{:S(2)}, u32[]{:S(2)}) async-start(bf16[16,120,128]{2,1,0:T(8,128)(2,1)} %broadcast_in_dim.30), calls=%async_computation.5 | async-start | bytes 983040 | tf_op jit(solution)/shard_map/all_to_all | solution.py:77
  373.9 22.6 %all-to-all-start.6 = ((bf16[16,48,768]{2,1,0:T(8,128)(2,1)}), bf16[16,48,768]{2,1,0:T(8,128)(2,1)}, u32[]{:S(2)}, u32[]{:S(2)}) async-start(bf16[16,48,768]{2,1,0:T(8,128)(2,1)} %bitcast.89), calls=%async_computation.6 | async-start | bytes 2359296 | tf_op jit(solution)/shard_map/all_to_all | solution.py:77
  380.0 3.2 collective-permute-start.9
  396.5 21.4 %all-to-all-start.7 = ((bf16[16,48,768]{2,1,0:T(8,128)(2,1)}), bf16[16,48,768]{2,1,0:T(8,128)(2,1)S(1)}, u32[]{:S(2)}, u32[]{:S(2)}) async-start(bf16[16,48,768]{2,1,0:T(8,128)(2,1)} %bitcast.97), calls=%async_computation.7 | async-start | bytes 2359296 | tf_op jit(solution)/shard_map/all_to_all | solution.py:77
  (81 other events, 380.9 us)
Sparse Core Ops, SparseCore 0:
  11.6 88.2 all-gather.1
